TPU v7x, 512 devices: a whole 4x4x16 slice. The times are simulated.
512 devices in a mesh: vocab: 64 (over z, y), tok: 8 (over x, core).
Axes of the slice: x: 4, y: 4, z: 16, core: 2. Of those that a mesh axis runs over, the one named last changes fastest.
Arguments:
- hidden: bfloat16 [1024, 3584], P('tok', 'vocab'), may hold values from -8 to 8
- head_weight: bfloat16 [3584, 81920], P('tok', 'vocab'), may hold values from -4 to 4
- targets: int32 [1024], P('tok'), may hold values from 0 to 81919
- response_mask: int32 [1024], P('tok'), may hold values 0 or 1
- labels: int32 [8], P('tok'), may hold values 0 or 1
- reference_sums: float32 [8, 2], P('tok'), may hold values from -48 to 48
Outputs:
- mean_loss: float32 [], replicated
- margins: float32 [8], P('tok')
- hidden_grad: bfloat16 [1024, 3584], P('tok', 'vocab')
- head_grad: bfloat16 [3584, 81920], P('tok', 'vocab')
All inputs are finite; a program needn't handle non-finite values. No bound on the sum of `response_mask` or of `labels` on one device may be relied on, other than what follows from the above.
Results may differ from a plain program's by a relative error of at most 0.0085.
Values may be sent and summed in bfloat16 or wider, within the bound.
A program may use at most 64 MiB of HBM per device.

v0:
```python
import math
import jax
import jax.numpy as jnp
from jax import lax
from jax.sharding import PartitionSpec as P

beta_scale = 0.1
tie_offset = math.log(2.0)
tie_const = math.log(3.0)
grad_scale = 512.0


def pair_terms(margins, labels):
    winner = labels.astype(jnp.float32)
    log_tie = (
        tie_const
        + margins
        - tie_offset
        - jax.nn.softplus(margins - tie_offset)
        - jax.nn.softplus(margins + tie_offset)
    )
    losses = winner * jax.nn.softplus(tie_offset - margins) - (1.0 - winner) * log_tie
    slopes = -winner * jax.nn.sigmoid(tie_offset - margins) - (1.0 - winner) * (
        1.0 - jax.nn.sigmoid(margins - tie_offset) - jax.nn.sigmoid(margins + tie_offset)
    )
    return (losses, slopes)


def local(hidden, head_weight, targets, response_mask, labels, reference_sums):
    tok_rows = hidden.shape[0]
    vocab_cols = head_weight.shape[1]
    tok_count = lax.axis_size("tok")
    pair_local = labels.shape[0]
    pair_total = pair_local * tok_count
    span = tok_rows // (2 * pair_local)
    rows_full = lax.all_gather(hidden, "vocab", axis=1, tiled=True)
    token_cols = lax.all_to_all(rows_full, "tok", split_axis=1, concat_axis=0, tiled=True)
    head_full = lax.all_gather(head_weight, "tok", axis=0, tiled=True)
    logits = jnp.dot(rows_full, head_full, preferred_element_type=jnp.float32)
    offset = lax.axis_index("vocab") * vocab_cols
    columns = lax.broadcasted_iota(jnp.int32, (1, vocab_cols), 1) + offset
    matched = columns == targets[:, None]
    local_max = jnp.max(logits, axis=1)
    local_target = jnp.sum(jnp.where(matched, logits, 0.0), axis=1)
    row_max = lax.pmax(local_max, "vocab")
    shifted = jnp.exp(logits - row_max[:, None])
    totals, target_logit = lax.psum((jnp.sum(shifted, axis=1), local_target), "vocab")
    probs = shifted / totals[:, None]
    token_logp = target_logit - (row_max + jnp.log(totals))
    weights = response_mask.astype(jnp.float32)
    sequence_logp = jnp.sum((token_logp * weights).reshape(pair_local, 2, span), axis=2)
    ratios = sequence_logp - reference_sums
    margins = beta_scale * (ratios[:, 0] - ratios[:, 1])
    losses, slopes = pair_terms(margins, labels)
    mean_loss = lax.psum(jnp.sum(losses), "tok") / pair_total
    pair_coef = beta_scale * grad_scale / pair_total * slopes
    signed = jnp.stack([pair_coef, -pair_coef], axis=1)
    token_coef = (
        jnp.broadcast_to(signed[:, :, None], (pair_local, 2, span)).reshape(tok_rows) * weights
    )
    onehot = jnp.where(matched, 1.0, 0.0).astype(jnp.float32)
    dlogits = (token_coef[:, None] * (onehot - probs)).astype(jnp.bfloat16)
    dlogit_all = lax.all_gather(dlogits, "tok", axis=0, tiled=True)
    head_grad = lax.dot_general(
        token_cols, dlogit_all, (((0,), (0,)), ((), ())), preferred_element_type=jnp.float32
    ).astype(jnp.bfloat16)
    grad_cols = lax.psum_scatter(
        lax.dot_general(
            head_full, dlogits, (((1,), (1,)), ((), ())), preferred_element_type=jnp.float32
        ),
        "vocab",
        scatter_dimension=0,
        tiled=True,
    )
    hidden_grad = grad_cols.T.astype(jnp.bfloat16)
    return (mean_loss, margins, hidden_grad, head_grad)


def solution(mesh):
    return jax.shard_map(
        local,
        mesh=mesh,
        in_specs=(
            P("tok", "vocab"),
            P("tok", "vocab"),
            P("tok"),
            P("tok"),
            P("tok"),
            P("tok", None),
        ),
        out_specs=(P(), P("tok"), P("tok", "vocab"), P("tok", "vocab")),
        check_vma=False,
    )
```

profile of v0, /device:TPU:6, one launch (start us, length us, event | category | flops | bytes accessed | tf_op | source)
XLA Modules:
  0.0 756.5 jit_solution(17143302099194967058)
XLA Ops:
  7.2 0.0 all-gather.3.cloned.1.call-start
  7.2 0.7 all-gather.3.cloned.1.call-update
  7.9 0.0 all-gather.5.cloned.1.call-start
  8.6 116.4 %all_gather.9 = bf16[128,3584]{0,1:T(8,128)(2,1)} all-gather(bf16[128,56]{0,1:T(8,128)(2,1)} %param.6), channel_id=1, replica_groups=mesh['vocab'=64,'tok'=8] {'vocab'}, dimensions={1}, use_global_device_ids=true | all-gather | bytes 931840 | tf_op jit(solution)/shard_map/all_gather | solution.py:36
  125.0 5.4 fusion.10
  130.4 140.4 %pmax.7 = f32[128]{0:T(128)S(1)} all-reduce(f32[128]{0:T(128)S(1)} %get-tuple-element.22), channel_id=1, replica_groups=mesh['vocab'=64,'tok'=8] {'vocab'}, use_global_device_ids=true, to_apply=%region_3.4 | all-reduce | flops 128 | bytes 1024 | tf_op jit(solution)/shard_map/pmax | solution.py:45
  270.9 0.3 fusion.7
  271.2 138.0 %all-reduce.1 = (f32[128]{0:T(128)S(1)}, f32[128]{0:T(128)S(1)}) all-reduce(f32[128]{0:T(128)S(1)} %get-tuple-element.17, f32[128]{0:T(128)S(1)} %get-tuple-element.16), channel_id=1, replica_groups=mesh['vocab'=64,'tok'=8] {'vocab'}, use_global_device_ids=true, to_apply=%region_1.2 | all-reduce | flops 256 | bytes 2048 | tf_op jit(solution)/shard_map/psum | solution.py:47
  409.2 0.1 reshape.33
  409.2 0.1 reduce_sum.37
  409.4 0.6 fusion.9
  411.5 0.1 maximum_bitcast_fusion
  411.6 0.1 broadcast_in_dim.26
  411.7 0.1 broadcast_in_dim.27
  411.8 1.0 fusion.6
  412.8 4.8 all-to-all-start
  417.6 1.3 dynamic-slice
  419.8 19.0 %psum.23 = f32[]{:T(128)} all-reduce(f32[]{:T(128)} %bitcast.2), channel_id=1, replica_groups=mesh['vocab'=64,'tok'=8] {'tok'}, use_global_device_ids=true, to_apply=%region_7.8 | all-reduce | flops 1 | bytes 8 | tf_op jit(solution)/shard_map/psum | solution.py:55
  438.8 6.9 convolution_bitcast_fusion
  445.7 295.8 %all-reduce.3 = bf16[3584,128]{0,1:T(8,128)(2,1)S(1)} all-reduce(f32[3584,128]{0,1:T(8,128)S(1)} %convolution_bitcast_fusion), channel_id=2, replica_groups=mesh['vocab'=64,'tok'=8] {'vocab'}, use_global_device_ids=true, to_apply=%region_8.9.clone | all-reduce | flops 458752 | bytes 2752512
  741.5 0.1 fusion.8
  741.6 0.7 copy.14
  743.0 0.0 all-gather.5.cloned.1.call-done
  743.0 4.4 fusion
  (13 shorter events, 0.1 us)
Async XLA Ops:
  7.2 117.9 %all-gather.3.cloned.1.call-start = ((), (), s32[]{:S(2)}) async-start(), calls=%async_computation.1 | async-start | bytes 10321920 | tf_op jit(solution)/shard_map/all_gather | solution.py:38
  7.9 735.1 %all-gather.5.cloned.1.call-start = ((), (), s32[]{:S(2)}) async-start(), calls=%async_computation.2 | async-start | bytes 2949120 | tf_op jit(solution)/shard_map/all_gather | solution.py:63
  125.0 145.9 %copy-start = (s32[128]{0:T(128)S(1)}, s32[128]{0:T(128)}, u32[]{:S(2)}) copy-start(s32[128]{0:T(128)} %param.8) | copy-start | bytes 1540
  125.0 284.1 %copy-start.1 = (s32[128]{0:T(128)S(1)}, s32[128]{0:T(128)}, u32[]{:S(2)}) copy-start(s32[128]{0:T(128)} %param.9) | copy-start | bytes 1540
  125.0 284.4 %copy-start.2 = (f32[1,2]{1,0:T(1,128)S(1)}, f32[1,2]{1,0:T(1,128)}, u32[]{:S(2)}) copy-start(f32[1,2]{1,0:T(1,128)} %param.11) | copy-start | bytes 28
  412.8 330.2 %all-to-all-start = ((bf16[128,8,448]{0,2,1:T(8,128)(2,1)}), bf16[128,8,448]{0,2,1:T(8,128)(2,1)}, u32[]{:S(2)}, u32[]{:S(2)}) async-start(bf16[128,8,448]{0,2,1:T(8,128)(2,1)} %bitcast.8), calls=%async_computation | async-start | bytes 1835008 | tf_op jit(solution)/shard_map/all_to_all | solution.py:37
Sparse Core Ops, SparseCore 0:
  10.1 63.2 all-gather.2
  412.9 30.2 all-gather.4
where the time goes:
time: 757 us; the launch traced here: 756 us
  blocking collectives  710 us (94%)
  between operations  20.2 us (3%)
  matrix products  16.6 us (2%)
    unnamed x1, blocking collectives  296 us
    pmax x1, blocking collectives, local(): row_max = lax.pmax(local_max, 'vocab')  140 us
    psum x1, blocking collectives, local(): lax.psum((jnp.sum(shifted, axis=1), local_target), 'vocab')  138 us
    all_gather x1, blocking collectives, local(): rows_full = lax.all_gather(hidden, 'vocab', axis=1, tiled=True)  116 us
    psum x1, blocking collectives, local(): mean_loss = lax.psum(jnp.sum(losses), 'tok') / pair_total  19 us
  transfers between devices with their start and end apart: 3, of which 0 were waited for; matrix products, arithmetic and copies ran while one was open for 1% of the time, Pallas kernels for 0%

commit v1 on v0

--- a/solution.py
+++ b/solution.py
@@ -8,6 +8,11 @@
 tie_offset = math.log(2.0)
 tie_const = math.log(3.0)
 grad_scale = 512.0
+
+
+def swapped_in(x, name, dim):
+    outgoing = jnp.stack([x] * lax.axis_size(name))
+    return jnp.concatenate(lax.all_to_all(outgoing, name, 0, 0), axis=dim)
 
 
 def pair_terms(margins, labels):
@@ -33,7 +38,7 @@
     pair_local = labels.shape[0]
     pair_total = pair_local * tok_count
     span = tok_rows // (2 * pair_local)
-    rows_full = lax.all_gather(hidden, "vocab", axis=1, tiled=True)
+    rows_full = swapped_in(hidden, "vocab", 1)
     token_cols = lax.all_to_all(rows_full, "tok", split_axis=1, concat_axis=0, tiled=True)
     head_full = lax.all_gather(head_weight, "tok", axis=0, tiled=True)
     logits = jnp.dot(rows_full, head_full, preferred_element_type=jnp.float32)

time: 757 us -> 714 us (0.943)
  blocking collectives: 710 us -> 596 us
  waiting for transfers between devices: 0.74 us -> 49.6 us
  starting transfers between devices: 4.91 us -> 25 us
    all_gather x1 -> x0, blocking collectives: 116 us -> none  [local(): rows_full = lax.all_gather(hidden, 'vocab', axis=1, tiled=True)]
    all_to_all x0 -> x1, waiting for transfers between devices: none -> 48.8 us  [swapped_in(): return jnp.concatenate(lax.all_to_all(outgoing, name, 0, 0), axis=dim)]
    all_to_all x0 -> x1, starting transfers between devices: none -> 19 us  [swapped_in(): return jnp.concatenate(lax.all_to_all(outgoing, name, 0, 0), axis=dim)]
  transfers between devices with their start and end apart: 3 -> 4, of which waited for: 0 -> 1; matrix products, arithmetic and copies ran while one was open for 1% -> 1% of each run, Pallas kernels for 0% -> 0%
where the time goes in v1:
time: 714 us; the launch traced here: 713 us
  blocking collectives  596 us (83%)
  waiting for transfers between devices  49.6 us (7%)
  starting transfers between devices  25 us (4%)
  between operations  20.2 us (3%)
  matrix products  16.6 us (2%)
    unnamed x1, blocking collectives  295 us
    pmax x1, blocking collectives, local(): row_max = lax.pmax(local_max, 'vocab')  140 us
    psum x1, blocking collectives, local(): lax.psum((jnp.sum(shifted, axis=1), local_target), 'vocab')  138 us
    all_to_all x1, waiting for transfers between devices, swapped_in(): return jnp.concatenate(lax.all_to_all(outgoing, name, 0, 0), axis=dim)  48.8 us
    psum x1, blocking collectives, local(): mean_loss = lax.psum(jnp.sum(losses), 'tok') / pair_total  22.9 us
    all_to_all x1, starting transfers between devices, swapped_in(): return jnp.concatenate(lax.all_to_all(outgoing, name, 0, 0), axis=dim)  19 us
  transfers between devices with their start and end apart: 4, of which 1 were waited for; matrix products, arithmetic and copies ran while one was open for 1% of the time, Pallas kernels for 0%

profile of v1, /device:TPU:6, one launch (start us, length us, event | category | flops | bytes accessed | tf_op | source)
XLA Modules:
  0.0 713.4 jit_solution(2390890864857348737)
XLA Ops:
  7.2 0.7 all-gather.3.cloned.1.call-update
  7.9 1.8 stack.8
  9.7 19.0 %all-to-all-start = ((bf16[64,128,56]{1,2,0:T(8,128)(2,1)}), bf16[64,128,56]{1,2,0:T(8,128)(2,1)}, u32[]{:S(2)}, u32[]{:S(2)}) async-start(bf16[64,128,56]{1,2,0:T(8,128)(2,1)} %stack.8), calls=%async_computation | async-start | bytes 1835008 | tf_op jit(solution)/shard_map/all_to_all | solution.py:15
  28.6 0.0 all-gather.5.cloned.1.call-start
  29.3 48.8 %all-to-all-done = bf16[64,128,56]{1,2,0:T(8,128)(2,1)} async-done(((bf16[64,128,56]{1,2,0:T(8,128)(2,1)}), bf16[64,128,56]{1,2,0:T(8,128)(2,1)}, u32[]{:S(2)}, u32[]{:S(2)}) %all-to-all-start) | async-done | bytes 917536 | tf_op jit(solution)/shard_map/all_to_all | solution.py:15
  78.2 5.4 fusion.10
  83.6 139.6 %pmax.7 = f32[128]{0:T(128)S(1)} all-reduce(f32[128]{0:T(128)S(1)} %get-tuple-element.22), channel_id=1, replica_groups=mesh['vocab'=64,'tok'=8] {'vocab'}, use_global_device_ids=true, to_apply=%region_3.4 | all-reduce | flops 128 | bytes 1024 | tf_op jit(solution)/shard_map/pmax | solution.py:50
  223.2 0.3 fusion.7
  223.5 138.4 %all-reduce.1 = (f32[128]{0:T(128)S(1)}, f32[128]{0:T(128)S(1)}) all-reduce(f32[128]{0:T(128)S(1)} %get-tuple-element.17, f32[128]{0:T(128)S(1)} %get-tuple-element.16), channel_id=1, replica_groups=mesh['vocab'=64,'tok'=8] {'vocab'}, use_global_device_ids=true, to_apply=%region_1.2 | all-reduce | flops 256 | bytes 2048 | tf_op jit(solution)/shard_map/psum | solution.py:52
  361.9 0.1 reshape.44
  362.0 0.1 reduce_sum.37
  362.1 0.6 fusion.9
  364.2 0.1 maximum_bitcast_fusion
  364.3 0.1 broadcast_in_dim.26
  364.4 0.1 broadcast_in_dim.27
  364.5 1.0 fusion.6
  365.5 1.3 dynamic-slice
  367.4 5.9 all-to-all-start.1
  373.6 22.9 %psum.23 = f32[]{:T(128)} all-reduce(f32[]{:T(128)} %bitcast.4), channel_id=1, replica_groups=mesh['vocab'=64,'tok'=8] {'tok'}, use_global_device_ids=true, to_apply=%region_7.8 | all-reduce | flops 1 | bytes 8 | tf_op jit(solution)/shard_map/psum | solution.py:60
  396.5 6.8 convolution_bitcast_fusion
  403.3 295.1 %all-reduce.3 = bf16[3584,128]{0,1:T(8,128)(2,1)S(1)} all-reduce(f32[3584,128]{0,1:T(8,128)S(1)} %convolution_bitcast_fusion), channel_id=2, replica_groups=mesh['vocab'=64,'tok'=8] {'vocab'}, use_global_device_ids=true, to_apply=%region_8.9.clone | all-reduce | flops 458752 | bytes 2752512
  698.4 0.1 fusion.8
  698.5 0.7 copy.15
  699.9 4.4 fusion
  (15 shorter events, 0.1 us)
Async XLA Ops:
  7.2 71.0 %all-gather.3.cloned.1.call-start = ((), (), s32[]{:S(2)}) async-start(), calls=%async_computation.2 | async-start | bytes 10321920 | tf_op jit(solution)/shard_map/all_gather | solution.py:43
  9.7 68.5 %all-to-all-start = ((bf16[64,128,56]{1,2,0:T(8,128)(2,1)}), bf16[64,128,56]{1,2,0:T(8,128)(2,1)}, u32[]{:S(2)}, u32[]{:S(2)}) async-start(bf16[64,128,56]{1,2,0:T(8,128)(2,1)} %stack.8), calls=%async_computation | async-start | bytes 1835008 | tf_op jit(solution)/shard_map/all_to_all | solution.py:15
  28.6 671.3 %all-gather.5.cloned.1.call-start = ((), (), s32[]{:S(2)}) async-start(), calls=%async_computation.3 | async-start | bytes 2949120 | tf_op jit(solution)/shard_map/all_gather | solution.py:68
  78.2 145.0 %copy-start = (s32[128]{0:T(128)S(1)}, s32[128]{0:T(128)}, u32[]{:S(2)}) copy-start(s32[128]{0:T(128)} %param.8) | copy-start | bytes 1540
  78.2 283.7 %copy-start.1 = (s32[128]{0:T(128)S(1)}, s32[128]{0:T(128)}, u32[]{:S(2)}) copy-start(s32[128]{0:T(128)} %param.9) | copy-start | bytes 1540
  78.2 283.9 %copy-start.2 = (f32[1,2]{1,0:T(1,128)S(1)}, f32[1,2]{1,0:T(1,128)}, u32[]{:S(2)}) copy-start(f32[1,2]{1,0:T(1,128)} %param.11) | copy-start | bytes 28
  367.4 332.5 %all-to-all-start.1 = ((bf16[128,8,448]{0,2,1:T(8,128)(2,1)}), bf16[128,8,448]{0,2,1:T(8,128)(2,1)}, u32[]{:S(2)}, u32[]{:S(2)}) async-start(bf16[128,8,448]{0,2,1:T(8,128)(2,1)} %bitcast.10), calls=%async_computation.1 | async-start | bytes 1835008 | tf_op jit(solution)/shard_map/all_to_all | solution.py:42
Sparse Core Ops, SparseCore 0:
  10.1 63.2 all-gather.2
  365.6 33.0 all-gather.4
